TPU v7x, 32 devices: a whole 2x2x4 slice. The times are simulated.
32 devices in a mesh: section: 2 (over core), ctx: 16 (over z, y, x).
Axes of the slice: x: 2, y: 2, z: 4, core: 2. Of those that a mesh axis runs over, the one named last changes fastest.
Arguments:
- projected: bfloat16 [2, 2048, 3, 2048], P('section', 'ctx'), may hold values from -6 to 6
- feat_taps: bfloat16 [2, 3, 3, 2048], P('section'), may hold values from -3 to 3
- skip_gain: float32 [2, 2048], P('section'), may hold values from -3 to 3
- long_filter: bfloat16 [2, 2048, 2048], P('section', 'ctx'), may hold values from -4 to 4
Outputs:
- handed: bfloat16 [2, 2048, 2048], P('section', 'ctx')
All inputs are finite; a program needn't handle non-finite values.
Results may differ from a plain program's by a relative error of at most 0.0068.
Values may be sent and summed in bfloat16 or wider, within the bound.
A program may use at most 128 MiB of HBM per device.

v0:
```python
import functools
import math

import jax
import jax.numpy as jnp
import ml_dtypes
import numpy as np
from jax import lax
from jax.experimental import pallas as pl
from jax.experimental.pallas import tpu as pltpu
from jax.sharding import PartitionSpec as P

GROUP = 16
MESH = pl.DeviceIdType.MESH


def tables(devices, length):
    total = devices * length
    r = np.arange(devices)
    p = np.arange(devices)
    s = np.arange(length)
    j = np.arange(length)
    short = np.exp(2j * np.pi * (((1 + 4 * r[:, None]) * p[None, :]) % (4 * devices)) / (4 * devices))
    phase = ((1 + 4 * r[:, None, None]) * j[None, None, :] + 4 * devices * s[None, :, None] * j[None, None, :]) % (4 * total)
    long = np.exp(2j * np.pi * phase / (4 * total))
    forward = np.concatenate(
        [np.concatenate([long.real, -long.imag], 2), np.concatenate([long.imag, long.real], 2)], 1
    )
    parts = np.stack([short.real, short.imag])
    return parts, forward


def two_terms(values):
    high = values.astype(ml_dtypes.bfloat16)
    low = (values - high.astype(np.float64)).astype(ml_dtypes.bfloat16)
    return high, low


def body_plain(projected, feat_taps, skip_gain, long_filter):
    devices = lax.axis_size("ctx")
    sections = lax.axis_size("section")
    streams = projected[0]
    length, _, channels = streams.shape
    share = channels // devices
    feat_count = feat_taps.shape[1]
    earlier = lax.ppermute(
        streams[length - (feat_count - 1) :], "ctx", [(i, i + 1) for i in range(devices - 1)]
    )
    extended = jnp.concatenate([earlier, streams], axis=0).astype(jnp.float32)
    featured = jnp.zeros((length, 3, channels), jnp.float32)
    for offset in range(feat_count):
        first = feat_count - 1 - offset
        featured = featured + feat_taps[0, offset].astype(jnp.float32) * extended[first : first + length]
    query = featured[:, 0]
    gated = featured[:, 1] * featured[:, 2]
    packed = jnp.stack([gated.astype(jnp.bfloat16), long_filter[0]])
    packed = packed.reshape(2, length, devices, share).transpose(2, 0, 1, 3)
    arrived = lax.all_to_all(packed, "ctx", split_axis=0, concat_axis=0, tiled=True)
    parts, forward = tables(devices, length)
    parts = jnp.asarray(parts, jnp.float32)
    forward = jnp.asarray(forward, jnp.float32)
    high = lax.Precision.HIGHEST
    blocks = arrived.astype(jnp.float32)
    partial = jnp.einsum("qrp,pkjc->krqjc", parts, blocks, precision=high)
    partial = partial.reshape(2, devices, 2 * length, share)
    spectrum = jnp.einsum("rxy,kryc->krxc", forward, partial, precision=high)
    data_re, data_im = spectrum[0, :, :length], spectrum[0, :, length:]
    filt_re, filt_im = spectrum[1, :, :length], spectrum[1, :, length:]
    product = jnp.concatenate(
        [data_re * filt_re - data_im * filt_im, data_re * filt_im + data_im * filt_re], 1
    )
    restored = jnp.einsum("rxy,rxc->ryc", forward, product, precision=high)
    restored = restored.reshape(devices, 2, length, share)
    conv = jnp.einsum("qrp,rqjc->pjc", parts, restored, precision=high) / (devices * length)
    back = lax.all_to_all(conv.astype(jnp.bfloat16), "ctx", split_axis=0, concat_axis=0, tiled=True)
    convolved = back.transpose(1, 0, 2).reshape(length, channels).astype(jnp.float32)
    output = (query * (convolved + skip_gain[0] * gated)).astype(jnp.bfloat16)
    return lax.ppermute(
        output[None], "section", [(i, (i + 1) % sections) for i in range(sections)]
    )


def partner(me, step, devices, arriving=False):
    if devices & (devices - 1) == 0:
        return me ^ step
    return lax.rem(me + (devices - step if arriving else step), devices)


def kernel(
    devices,
    sections,
    streams_ref,
    taps_ref,
    skip_ref,
    filter_ref,
    short_ref,
    back_ref,
    long_ref,
    longback_ref,
    out_ref,
    streams,
    short,
    back,
    long,
    longback,
    tail,
    halo,
    gated_out,
    query,
    skipped,
    filter_in,
    gated_in,
    query_in,
    skipped_in,
    partial,
    spectrum,
    restored,
    conv,
    conv_in,
    local_sem,
    halo_sem,
    filter_send,
    filter_recv,
    gated_send,
    gated_recv,
    cross_sem,
    conv_send,
    conv_recv,
):
    me = lax.axis_index("ctx")
    beyond = lax.rem(lax.axis_index("section") + 1, sections)
    length, channels = filter_ref.shape
    share = channels // devices
    feat_count = taps_ref.shape[0] // 3
    keep = feat_count - 1
    rows = devices * GROUP

    def lanes(index):
        return pl.ds(pl.multiple_of(index * share, share), share)

    def filter_copy(step):
        to = partner(me, step, devices)
        return pltpu.make_async_remote_copy(
            src_ref=filter_ref.at[:, lanes(to)],
            dst_ref=filter_in.at[me],
            send_sem=filter_send.at[step],
            recv_sem=filter_recv.at[step],
            device_id={"ctx": to},
            device_id_type=MESH,
        )

    def gated_copy(step):
        to = partner(me, step, devices)
        return pltpu.make_async_remote_copy(
            src_ref=gated_out.at[to],
            dst_ref=gated_in.at[me],
            send_sem=gated_send.at[step],
            recv_sem=gated_recv.at[step],
            device_id={"ctx": to},
            device_id_type=MESH,
        )

    def conv_copy(step):
        to = partner(me, step, devices)
        return pltpu.make_async_remote_copy(
            src_ref=conv.at[to],
            dst_ref=conv_in.at[me],
            send_sem=conv_send.at[step],
            recv_sem=conv_recv.at[step],
            device_id={"ctx": to, "section": beyond},
            device_id_type=MESH,
        )

    def cross_copy(index, source, target):
        return pltpu.make_async_remote_copy(
            src_ref=source,
            dst_ref=target,
            send_sem=cross_sem.at[2 * index],
            recv_sem=cross_sem.at[2 * index + 1],
            device_id={"section": beyond},
            device_id_type=MESH,
        )

    halo_copy = pltpu.make_async_remote_copy(
        src_ref=tail,
        dst_ref=halo,
        send_sem=halo_sem.at[0],
        recv_sem=halo_sem.at[1],
        device_id={"ctx": lax.rem(me + 1, devices)},
        device_id_type=MESH,
    )
    load_streams = pltpu.make_async_copy(streams_ref, streams, local_sem.at[0])
    own_filter = pltpu.make_async_copy(filter_ref.at[:, lanes(me)], filter_in.at[me], local_sem.at[1])
    loads = [
        pltpu.make_async_copy(source, target, local_sem.at[2 + i])
        for i, (source, target) in enumerate(
            [(short_ref, short), (long_ref, long), (longback_ref, longback), (back_ref, back)]
        )
    ]

    load_streams.start()

    @pl.loop(0, devices - 1)
    def _(i):
        filter_copy(devices - 1 - i).start()

    own_filter.start()
    load_streams.wait()
    for copy in loads:
        copy.start()

    for stream in range(3):
        last = streams[stream, length - GROUP :, :].astype(jnp.float32)
        tail[stream * keep : (stream + 1) * keep, :] = last[GROUP - keep :, :]
    if tail.shape[0] > 3 * keep:
        tail[3 * keep :, :] = jnp.zeros((tail.shape[0] - 3 * keep, channels), jnp.float32)

    @pl.when(me < devices - 1)
    def _():
        halo_copy.start()

    @pl.when(me > 0)
    def _():
        halo_copy.wait_recv()

    @pl.when(me == 0)
    def _():
        halo[...] = jnp.zeros_like(halo)

    row_ids = lax.broadcasted_iota(jnp.int32, (length, share), 0)

    def features(index):
        at = lanes(index)
        found = []
        for stream in range(3):
            values = streams[stream, :, at].astype(jnp.float32)
            total = taps_ref[pl.ds(stream, 1), at] * values
            for offset in range(1, feat_count):
                moved = pltpu.roll(values, offset, 0)
                for row in range(offset):
                    before = halo[pl.ds(stream * keep + keep - offset + row, 1), at]
                    moved = jnp.where(row_ids == row, before, moved)
                total = total + taps_ref[pl.ds(offset * 3 + stream, 1), at] * moved
            found.append(total)
        gated = found[1] * found[2]
        gated_out[index] = gated.astype(jnp.bfloat16)
        query[index] = found[0]
        skipped[index] = skip_ref[:, at] * gated

    @pl.loop(0, devices - 1)
    def _(i):
        step = devices - 1 - i
        features(partner(me, step, devices))
        gated_copy(step).start()

    features(me)
    gated_in[me] = gated_out[me]
    cross_copy(0, query, query_in).start()
    cross_copy(1, skipped, skipped_in).start()

    def short_transform(arrived):
        @pl.loop(0, length // GROUP)
        def _(g):
            at = pl.ds(pl.multiple_of(g * GROUP, GROUP), GROUP)
            values = arrived[:, at, :].reshape(rows, share)
            done = jnp.dot(short[0], values, preferred_element_type=jnp.float32)
            done = done + jnp.dot(short[1], values, preferred_element_type=jnp.float32)
            done = done.astype(jnp.bfloat16).reshape(2, devices, GROUP, share)
            partial[:, at, :] = done[0]
            partial[:, pl.ds(pl.multiple_of(length + g * GROUP, GROUP), GROUP), :] = done[1]

    own_filter.wait()

    @pl.loop(0, devices - 1)
    def _(i):
        filter_copy(devices - 1 - i).wait_recv()

    for copy in loads:
        copy.wait()
    short_transform(filter_in)

    @pl.loop(0, devices)
    def _(r):
        spectrum[r] = jnp.dot(long[r], partial[r], preferred_element_type=jnp.float32)

    @pl.loop(0, devices - 1)
    def _(i):
        gated_copy(devices - 1 - i).wait_recv()

    short_transform(gated_in)

    @pl.loop(0, devices)
    def _(r):
        data = jnp.dot(long[r], partial[r], preferred_element_type=jnp.float32)
        data_re, data_im = data[:length], data[length:]
        filt_re, filt_im = spectrum[r, :length], spectrum[r, length:]
        product = jnp.concatenate(
            [data_re * filt_re - data_im * filt_im, data_re * filt_im + data_im * filt_re], 0
        )
        restored[r] = jnp.dot(
            longback[r], product.astype(jnp.bfloat16), preferred_element_type=jnp.float32
        ).astype(jnp.bfloat16)

    @pl.loop(0, length // GROUP)
    def _(g):
        at = pl.ds(pl.multiple_of(g * GROUP, GROUP), GROUP)
        real = restored[:, at, :].reshape(rows, share)
        imag = restored[:, pl.ds(pl.multiple_of(length + g * GROUP, GROUP), GROUP), :].reshape(rows, share)
        values = jnp.concatenate([real, imag], 0)
        done = jnp.dot(back[0], values, preferred_element_type=jnp.float32)
        done = done + jnp.dot(back[1], values, preferred_element_type=jnp.float32)
        conv[:, at, :] = done.astype(jnp.bfloat16).reshape(devices, GROUP, share)

    @pl.loop(0, devices)
    def _(i):
        conv_copy(devices - 1 - i).start()

    cross_copy(0, query, query_in).wait()
    cross_copy(1, skipped, skipped_in).wait()

    @pl.when(me < devices - 1)
    def _():
        halo_copy.wait_send()

    @pl.loop(0, devices - 1)
    def _(i):
        filter_copy(devices - 1 - i).wait_send()
        gated_copy(devices - 1 - i).wait_send()

    @pl.loop(0, devices)
    def _(i):
        step = lax.rem(i, devices)
        conv_copy(step).wait_recv()
        source = partner(me, step, devices, arriving=True)
        mixed = query_in[source] * (conv_in[source].astype(jnp.float32) + skipped_in[source])
        out_ref[:, lanes(source)] = mixed.astype(jnp.bfloat16)

    @pl.loop(0, devices)
    def _(i):
        conv_copy(i).wait_send()


def body_kernel(projected, feat_taps, skip_gain, long_filter):
    devices = lax.axis_size("ctx")
    sections = lax.axis_size("section")
    streams = jnp.transpose(projected[0], (1, 0, 2))
    _, length, channels = streams.shape
    share = channels // devices
    feat_count = feat_taps.shape[1]
    taps = feat_taps[0].astype(jnp.float32).reshape(feat_count * 3, channels)
    parts, forward = tables(devices, length)
    eye = np.eye(GROUP)
    short = np.einsum("qrp,ab->qrapb", parts, eye).reshape(2 * devices * GROUP, devices * GROUP)
    short_pair = np.stack(two_terms(short))
    back_pair = np.stack(two_terms(short.T / (devices * length)))
    long = forward.astype(ml_dtypes.bfloat16)
    longback = np.ascontiguousarray(forward.transpose(0, 2, 1)).astype(ml_dtypes.bfloat16)
    tail_rows = -(-3 * (feat_count - 1) // 8) * 8
    bf16, f32 = jnp.bfloat16, jnp.float32
    dma = pltpu.SemaphoreType.DMA
    anywhere = pl.BlockSpec(memory_space=pl.ANY)
    whole = pl.BlockSpec(memory_space=pltpu.VMEM)
    call = pl.pallas_call(
        functools.partial(kernel, devices, sections),
        out_shape=jax.ShapeDtypeStruct((length, channels), bf16),
        in_specs=[anywhere, whole, whole, anywhere, anywhere, anywhere, anywhere, anywhere],
        out_specs=whole,
        scratch_shapes=[
            pltpu.VMEM((3, length, channels), bf16),
            pltpu.VMEM(short_pair.shape, bf16),
            pltpu.VMEM(back_pair.shape, bf16),
            pltpu.VMEM(long.shape, bf16),
            pltpu.VMEM(longback.shape, bf16),
            pltpu.VMEM((tail_rows, channels), f32),
            pltpu.VMEM((tail_rows, channels), f32),
            pltpu.VMEM((devices, length, share), bf16),
            pltpu.VMEM((devices, length, share), f32),
            pltpu.VMEM((devices, length, share), f32),
            pltpu.VMEM((devices, length, share), bf16),
            pltpu.VMEM((devices, length, share), bf16),
            pltpu.VMEM((devices, length, share), f32),
            pltpu.VMEM((devices, length, share), f32),
            pltpu.VMEM((devices, 2 * length, share), bf16),
            pltpu.VMEM((devices, 2 * length, share), f32),
            pltpu.VMEM((devices, 2 * length, share), bf16),
            pltpu.VMEM((devices, length, share), bf16),
            pltpu.VMEM((devices, length, share), bf16),
            dma((6,)),
            dma((2,)),
            dma((devices,)),
            dma((devices,)),
            dma((devices,)),
            dma((devices,)),
            dma((4,)),
            dma((devices,)),
            dma((devices,)),
        ],
        compiler_params=pltpu.CompilerParams(has_side_effects=True, vmem_limit_bytes=48 * 1024 * 1024),
        name="mixer",
    )
    out = call(
        streams,
        taps,
        skip_gain,
        long_filter[0],
        jnp.asarray(short_pair),
        jnp.asarray(back_pair),
        jnp.asarray(long),
        jnp.asarray(longback),
    )
    return out[None]


def solution(mesh):
    devices, sections = mesh.shape["ctx"], mesh.shape["section"]

    def body(projected, feat_taps, skip_gain, long_filter):
        _, length, channels = long_filter.shape
        feat_count = feat_taps.shape[1]
        fits = channels % (128 * devices) == 0 and length % 128 == 0
        fits = fits and sections > 1 and devices > 1 and feat_count - 1 <= GROUP
        run = body_kernel if fits else body_plain
        return run(projected, feat_taps, skip_gain, long_filter)

    return jax.shard_map(
        body,
        mesh=mesh,
        in_specs=(
            P("section", "ctx", None, None),
            P("section", None, None, None),
            P("section", None),
            P("section", "ctx", None),
        ),
        out_specs=P("section", "ctx", None),
        check_vma=False,
    )
```

profile of v0, /device:TPU:0, one launch (start us, length us, event | category | flops | bytes accessed | tf_op | source)
XLA Modules:
  0.0 69.2 jit_solution(10915892349687503728)
XLA Ops:
  0.0 0.8 %reshape.4.taps_ref = f32[9,2048]{1,0:T(8,128)S(1)} reshape(bf16[1,3,3,2048]{3,2,1,0:T(4,128)(2,1)} %param.9) | data formatting | bytes 110592 | tf_op jit(solution)/shard_map/convert_element_type | solution.py:350
  0.8 0.0 copy-start
  0.8 1.6 %copy-done = bf16[16,256,256]{2,1,0:T(8,128)(2,1)S(1)} copy-done((bf16[16,256,256]{2,1,0:T(8,128)(2,1)S(1)}, bf16[16,256,256]{2,1,0:T(8,128)(2,1)}, u32[]{:S(2)}) %copy-start) | copy-done | bytes 2097176
  2.4 0.0 copy-start.1
  2.4 1.4 %copy-done.1 = bf16[1,128,3,2048]{3,1,2,0:T(8,128)(2,1)S(1)} copy-done((bf16[1,128,3,2048]{3,1,2,0:T(8,128)(2,1)S(1)}, bf16[1,128,3,2048]{3,1,2,0:T(8,128)(2,1)}, u32[]{:S(2)}) %copy-start.1) | copy-done | bytes 1572888
  3.8 0.0 copy-start.2
  3.8 1.0 %copy-done.2 = bf16[1,128,2048]{2,1,0:T(8,128)(2,1)S(1)} copy-done((bf16[1,128,2048]{2,1,0:T(8,128)(2,1)S(1)}, bf16[1,128,2048]{2,1,0:T(8,128)(2,1)}, u32[]{:S(2)}) %copy-start.2) | copy-done | bytes 524312
  4.9 0.0 copy-start.3
  4.9 1.0 %copy-done.3 = bf16[2,256,512]{2,1,0:T(8,128)(2,1)S(1)} copy-done((bf16[2,256,512]{2,1,0:T(8,128)(2,1)S(1)}, bf16[2,256,512]{2,1,0:T(8,128)(2,1)}, u32[]{:S(2)}) %copy-start.3) | copy-done | bytes 524312
  5.9 0.0 copy-start.4
  5.9 1.0 %copy-done.4 = bf16[2,512,256]{2,1,0:T(8,128)(2,1)S(1)} copy-done((bf16[2,512,256]{2,1,0:T(8,128)(2,1)S(1)}, bf16[2,512,256]{2,1,0:T(8,128)(2,1)}, u32[]{:S(2)}) %copy-start.4) | copy-done | bytes 524312
  7.0 0.0 copy-start.5
  7.0 0.7 %copy-done.5 = f32[1,2048]{1,0:T(1,128)S(1)} copy-done((f32[1,2048]{1,0:T(1,128)S(1)}, f32[1,2048]{1,0:T(1,128)}, u32[]{:S(2)}) %copy-start.5) | copy-done | bytes 8216
  7.7 60.7 %mixer.1 = bf16[128,2048]{1,0:T(8,128)(2,1)S(1)} custom-call(bf16[3,128,2048]{2,1,0:T(8,128)(2,1)S(1)} %bitcast.6, f32[9,2048]{1,0:T(8,128)S(1)} %reshape.4.taps_ref, f32[1,2048]{1,0:T(1,128)S(1)} %copy-done.5, bf16[128,2048]{1,0:T(8,128)(2,1)S(1)} %bitcast.7, bf16[2,512,256]{2,1,0:T(8,128)(2,1)S(1)} %copy-done.4, bf16[2,256,512]{2,1,0:T(8,128)(2,1)S(1)} %copy-done.3, ...), custom_call_target="tpu_custom_call" | custom-call | tf_op jit(solution)/shard_map/mixer/pallas_call | solution.py:401
  68.4 0.8 %copy.10 = bf16[1,128,2048]{2,1,0:T(8,128)(2,1)} copy(bf16[1,128,2048]{2,1,0:T(8,128)(2,1)S(1)} %bitcast.5) | data formatting | bytes 1048576
Async XLA Ops:
  0.8 1.6 %copy-start = (bf16[16,256,256]{2,1,0:T(8,128)(2,1)S(1)}, bf16[16,256,256]{2,1,0:T(8,128)(2,1)}, u32[]{:S(2)}) copy-start(bf16[16,256,256]{2,1,0:T(8,128)(2,1)} %constant.10.clone.long_ref) | copy-start | bytes 6291460
  2.4 1.4 %copy-start.1 = (bf16[1,128,3,2048]{3,1,2,0:T(8,128)(2,1)S(1)}, bf16[1,128,3,2048]{3,1,2,0:T(8,128)(2,1)}, u32[]{:S(2)}) copy-start(bf16[1,128,3,2048]{3,1,2,0:T(8,128)(2,1)} %param.8) | copy-start | bytes 4718596
  3.8 1.0 %copy-start.2 = (bf16[1,128,2048]{2,1,0:T(8,128)(2,1)S(1)}, bf16[1,128,2048]{2,1,0:T(8,128)(2,1)}, u32[]{:S(2)}) copy-start(bf16[1,128,2048]{2,1,0:T(8,128)(2,1)} %param.11) | copy-start | bytes 1572868
  4.9 1.0 %copy-start.3 = (bf16[2,256,512]{2,1,0:T(8,128)(2,1)S(1)}, bf16[2,256,512]{2,1,0:T(8,128)(2,1)}, u32[]{:S(2)}) copy-start(bf16[2,256,512]{2,1,0:T(8,128)(2,1)} %constant.9.clone.back_ref) | copy-start | bytes 1572868
  5.9 1.0 %copy-start.4 = (bf16[2,512,256]{2,1,0:T(8,128)(2,1)S(1)}, bf16[2,512,256]{2,1,0:T(8,128)(2,1)}, u32[]{:S(2)}) copy-start(bf16[2,512,256]{2,1,0:T(8,128)(2,1)} %constant.8.clone.short_ref) | copy-start | bytes 1572868
  7.0 0.7 %copy-start.5 = (f32[1,2048]{1,0:T(1,128)S(1)}, f32[1,2048]{1,0:T(1,128)}, u32[]{:S(2)}) copy-start(f32[1,2048]{1,0:T(1,128)} %skip_ref.1) | copy-start | bytes 24580
where the time goes:
time: 69.6 us; the launch traced here: 69.2 us
  Pallas kernels  60.7 us (87%)
  local copies, waits for them, and re-layouts  8.44 us (12%)
    pallas_call x1, Pallas kernels, body_kernel(): call(streams, taps, skip_gain, long_filter[0], jnp.asarray(short_pair), j...  60.7 us
    unnamed x13, local copies, waits for them, and re-layouts  7.61 us

commit v1 on v0

--- a/solution.py
+++ b/solution.py
@@ -99,6 +99,9 @@
     longback_ref,
     out_ref,
     streams,
+    taps_raw,
+    taps,
+    skip,
     short,
     back,
     long,
@@ -131,7 +134,7 @@
     beyond = lax.rem(lax.axis_index("section") + 1, sections)
     length, channels = filter_ref.shape
     share = channels // devices
-    feat_count = taps_ref.shape[0] // 3
+    feat_count = taps_ref.shape[0]
     keep = feat_count - 1
     rows = devices * GROUP
 
@@ -197,17 +200,41 @@
             [(short_ref, short), (long_ref, long), (longback_ref, longback), (back_ref, back)]
         )
     ]
+    load_taps = pltpu.make_async_copy(taps_ref, taps_raw, local_sem.at[6])
+    load_skip = pltpu.make_async_copy(skip_ref, skip, local_sem.at[7])
+
+    barrier = pltpu.get_barrier_semaphore()
+    before = lax.rem(lax.axis_index("section") + sections - 1, sections)
+    others = [beyond] if sections == 2 else [beyond, before]
+
+    @pl.loop(1, devices)
+    def _(step):
+        pl.semaphore_signal(
+            barrier, inc=1, device_id={"ctx": lax.rem(me + step, devices)}, device_id_type=MESH
+        )
+
+    for other in others:
+
+        @pl.loop(0, devices)
+        def _(step):
+            pl.semaphore_signal(
+                barrier,
+                inc=1,
+                device_id={"ctx": lax.rem(me + step, devices), "section": other},
+                device_id_type=MESH,
+            )
 
     load_streams.start()
-
-    @pl.loop(0, devices - 1)
-    def _(i):
-        filter_copy(devices - 1 - i).start()
-
-    own_filter.start()
+    load_taps.start()
+    load_skip.start()
+    pl.semaphore_wait(barrier, devices - 1 + len(others) * devices)
+    ahead = min(3, devices - 1)
+
+    @pl.loop(0, ahead)
+    def _(i):
+        filter_copy(1 + i).start()
+
     load_streams.wait()
-    for copy in loads:
-        copy.start()
 
     for stream in range(3):
         last = streams[stream, length - GROUP :, :].astype(jnp.float32)
@@ -219,6 +246,18 @@
     def _():
         halo_copy.start()
 
+    @pl.loop(ahead, devices - 1)
+    def _(i):
+        filter_copy(1 + i).start()
+
+    own_filter.start()
+    for copy in loads:
+        copy.start()
+    load_taps.wait()
+    load_skip.wait()
+    for offset in range(feat_count):
+        taps[offset] = taps_raw[offset].astype(jnp.float32)
+
     @pl.when(me > 0)
     def _():
         halo_copy.wait_recv()
@@ -234,22 +273,22 @@
         found = []
         for stream in range(3):
             values = streams[stream, :, at].astype(jnp.float32)
-            total = taps_ref[pl.ds(stream, 1), at] * values
+            total = taps[0, pl.ds(stream, 1), at] * values
             for offset in range(1, feat_count):
                 moved = pltpu.roll(values, offset, 0)
                 for row in range(offset):
                     before = halo[pl.ds(stream * keep + keep - offset + row, 1), at]
                     moved = jnp.where(row_ids == row, before, moved)
-                total = total + taps_ref[pl.ds(offset * 3 + stream, 1), at] * moved
+                total = total + taps[offset, pl.ds(stream, 1), at] * moved
             found.append(total)
         gated = found[1] * found[2]
         gated_out[index] = gated.astype(jnp.bfloat16)
         query[index] = found[0]
-        skipped[index] = skip_ref[:, at] * gated
+        skipped[index] = skip[:, at] * gated
 
     @pl.loop(0, devices - 1)
     def _(i):
-        step = devices - 1 - i
+        step = 1 + i
         features(partner(me, step, devices))
         gated_copy(step).start()
 
@@ -258,38 +297,45 @@
     cross_copy(0, query, query_in).start()
     cross_copy(1, skipped, skipped_in).start()
 
+    def group(g, first=0):
+        start = first + g * GROUP
+        return pl.ds(start if isinstance(start, int) else pl.multiple_of(start, GROUP), GROUP)
+
+    def two_dots(table, values):
+        done = jnp.dot(table[0], values, preferred_element_type=jnp.float32)
+        return done + jnp.dot(table[1], values, preferred_element_type=jnp.float32)
+
     def short_transform(arrived):
-        @pl.loop(0, length // GROUP)
+        @pl.loop(0, length // GROUP, step=2, unroll=length // (2 * GROUP))
         def _(g):
-            at = pl.ds(pl.multiple_of(g * GROUP, GROUP), GROUP)
-            values = arrived[:, at, :].reshape(rows, share)
-            done = jnp.dot(short[0], values, preferred_element_type=jnp.float32)
-            done = done + jnp.dot(short[1], values, preferred_element_type=jnp.float32)
-            done = done.astype(jnp.bfloat16).reshape(2, devices, GROUP, share)
-            partial[:, at, :] = done[0]
-            partial[:, pl.ds(pl.multiple_of(length + g * GROUP, GROUP), GROUP), :] = done[1]
+            values = [arrived[:, group(g + i), :].reshape(rows, share) for i in range(2)]
+            done = two_dots(short, jnp.concatenate(values, 1)).astype(jnp.bfloat16)
+            for i in range(2):
+                part = done[:, i * share : (i + 1) * share].reshape(2, devices, GROUP, share)
+                partial[:, group(g + i), :] = part[0]
+                partial[:, group(g + i, length), :] = part[1]
 
     own_filter.wait()
 
     @pl.loop(0, devices - 1)
     def _(i):
-        filter_copy(devices - 1 - i).wait_recv()
+        filter_copy(1 + i).wait_recv()
 
     for copy in loads:
         copy.wait()
     short_transform(filter_in)
 
-    @pl.loop(0, devices)
+    @pl.loop(0, devices, unroll=devices)
     def _(r):
         spectrum[r] = jnp.dot(long[r], partial[r], preferred_element_type=jnp.float32)
 
     @pl.loop(0, devices - 1)
     def _(i):
-        gated_copy(devices - 1 - i).wait_recv()
+        gated_copy(1 + i).wait_recv()
 
     short_transform(gated_in)
 
-    @pl.loop(0, devices)
+    @pl.loop(0, devices, unroll=devices)
     def _(r):
         data = jnp.dot(long[r], partial[r], preferred_element_type=jnp.float32)
         data_re, data_im = data[:length], data[length:]
@@ -301,19 +347,23 @@
             longback[r], product.astype(jnp.bfloat16), preferred_element_type=jnp.float32
         ).astype(jnp.bfloat16)
 
-    @pl.loop(0, length // GROUP)
+    @pl.loop(0, length // GROUP, step=2, unroll=length // (2 * GROUP))
     def _(g):
-        at = pl.ds(pl.multiple_of(g * GROUP, GROUP), GROUP)
-        real = restored[:, at, :].reshape(rows, share)
-        imag = restored[:, pl.ds(pl.multiple_of(length + g * GROUP, GROUP), GROUP), :].reshape(rows, share)
-        values = jnp.concatenate([real, imag], 0)
-        done = jnp.dot(back[0], values, preferred_element_type=jnp.float32)
-        done = done + jnp.dot(back[1], values, preferred_element_type=jnp.float32)
-        conv[:, at, :] = done.astype(jnp.bfloat16).reshape(devices, GROUP, share)
-
-    @pl.loop(0, devices)
-    def _(i):
-        conv_copy(devices - 1 - i).start()
+        values = [
+            jnp.concatenate(
+                [restored[:, group(g + i, first), :].reshape(rows, share) for first in (0, length)], 0
+            )
+            for i in range(2)
+        ]
+        done = two_dots(back, jnp.concatenate(values, 1)).astype(jnp.bfloat16)
+        for i in range(2):
+            conv[:, group(g + i), :] = done[:, i * share : (i + 1) * share].reshape(devices, GROUP, share)
+
+    @pl.loop(1, devices)
+    def _(step):
+        conv_copy(step).start()
+
+    conv_copy(0).start()
 
     cross_copy(0, query, query_in).wait()
     cross_copy(1, skipped, skipped_in).wait()
@@ -324,12 +374,12 @@
 
     @pl.loop(0, devices - 1)
     def _(i):
-        filter_copy(devices - 1 - i).wait_send()
-        gated_copy(devices - 1 - i).wait_send()
+        filter_copy(1 + i).wait_send()
+        gated_copy(1 + i).wait_send()
 
     @pl.loop(0, devices)
     def _(i):
-        step = lax.rem(i, devices)
+        step = lax.rem(i + 1, devices)
         conv_copy(step).wait_recv()
         source = partner(me, step, devices, arriving=True)
         mixed = query_in[source] * (conv_in[source].astype(jnp.float32) + skipped_in[source])
@@ -347,7 +397,6 @@
     _, length, channels = streams.shape
     share = channels // devices
     feat_count = feat_taps.shape[1]
-    taps = feat_taps[0].astype(jnp.float32).reshape(feat_count * 3, channels)
     parts, forward = tables(devices, length)
     eye = np.eye(GROUP)
     short = np.einsum("qrp,ab->qrapb", parts, eye).reshape(2 * devices * GROUP, devices * GROUP)
@@ -358,15 +407,18 @@
     tail_rows = -(-3 * (feat_count - 1) // 8) * 8
     bf16, f32 = jnp.bfloat16, jnp.float32
     dma = pltpu.SemaphoreType.DMA
-    anywhere = pl.BlockSpec(memory_space=pl.ANY)
+    stays = pl.BlockSpec(memory_space=pltpu.HBM)
     whole = pl.BlockSpec(memory_space=pltpu.VMEM)
     call = pl.pallas_call(
         functools.partial(kernel, devices, sections),
         out_shape=jax.ShapeDtypeStruct((length, channels), bf16),
-        in_specs=[anywhere, whole, whole, anywhere, anywhere, anywhere, anywhere, anywhere],
+        in_specs=[stays] * 8,
         out_specs=whole,
         scratch_shapes=[
             pltpu.VMEM((3, length, channels), bf16),
+            pltpu.VMEM((feat_count, 3, channels), bf16),
+            pltpu.VMEM((feat_count, 3, channels), f32),
+            pltpu.VMEM((1, channels), f32),
             pltpu.VMEM(short_pair.shape, bf16),
             pltpu.VMEM(back_pair.shape, bf16),
             pltpu.VMEM(long.shape, bf16),
@@ -385,7 +437,7 @@
             pltpu.VMEM((devices, 2 * length, share), bf16),
             pltpu.VMEM((devices, length, share), bf16),
             pltpu.VMEM((devices, length, share), bf16),
-            dma((6,)),
+            dma((8,)),
             dma((2,)),
             dma((devices,)),
             dma((devices,)),
@@ -395,12 +447,12 @@
             dma((devices,)),
             dma((devices,)),
         ],
-        compiler_params=pltpu.CompilerParams(has_side_effects=True, vmem_limit_bytes=48 * 1024 * 1024),
+        compiler_params=pltpu.CompilerParams(collective_id=0, has_side_effects=True, vmem_limit_bytes=127 * 512 * 1024),
         name="mixer",
     )
     out = call(
         streams,
-        taps,
+        feat_taps[0],
         skip_gain,
         long_filter[0],
         jnp.asarray(short_pair),

time: 69.6 us -> 50.7 us (0.73)
  Pallas kernels: 60.7 us -> 47.9 us
  local copies, waits for them, and re-layouts: 8.44 us -> 1.88 us
    pallas_call x1, Pallas kernels: 60.7 us -> 47.9 us  [body_kernel(): call(streams, feat_taps[0], skip_gain, long_filter[0], jnp.asarray(short_...]
    unnamed x13 -> x1, local copies, waits for them, and re-layouts: 7.61 us -> 1.88 us
    convert_element_type x1 -> x0, local copies, waits for them, and re-layouts: 0.83 us -> none  [body_kernel(): taps = feat_taps[0].astype(jnp.float32).reshape(feat_count * 3, channels)]
where the time goes in v1:
time: 50.7 us; the launch traced here: 49.8 us
  Pallas kernels  47.9 us (94%)
  local copies, waits for them, and re-layouts  1.88 us (4%)
    pallas_call x1, Pallas kernels, body_kernel(): call(streams, feat_taps[0], skip_gain, long_filter[0], jnp.asarray(short_...  47.9 us
    unnamed x1, local copies, waits for them, and re-layouts  1.88 us

profile of v1, /device:TPU:0, one launch (start us, length us, event | category | flops | bytes accessed | tf_op | source)
XLA Modules:
  0.0 49.8 jit_solution(12204654246474551676)
XLA Ops:
  0.0 47.9 %mixer.1 = bf16[128,2048]{1,0:T(8,128)(2,1)} custom-call(bf16[3,128,2048]{2,1,0:T(8,128)(2,1)} %bitcast.7, bf16[3,3,2048]{2,1,0:T(4,128)(2,1)} %bitcast.9, f32[1,2048]{1,0:T(1,128)} %skip_ref.1, bf16[128,2048]{1,0:T(8,128)(2,1)} %bitcast.8, bf16[2,512,256]{2,1,0:T(8,128)(2,1)} %constant.8.clone.short_ref, bf16[2,256,512]{2,1,0:T(8,128)(2,1)} %constant.9.clone.back_ref, ...), custom_call_target="tpu_custom_call" | custom-call | tf_op jit(solution)/shard_map/mixer/pallas_call | solution.py:453
  48.0 1.9 %copy.10 = bf16[1,128,2048]{2,1,0:T(8,128)(2,1)} copy(bf16[1,128,2048]{2,1,0:T(8,128)(2,1)} %bitcast.6) | data formatting | bytes 1048576

commit v2 on v1

--- a/solution.py
+++ b/solution.py
@@ -84,6 +84,23 @@
     if devices & (devices - 1) == 0:
         return me ^ step
     return lax.rem(me + (devices - step if arriving else step), devices)
+
+
+def bit_sum(value, devices):
+    total, size = value, 1
+    while 1 << size < devices:
+        total = total ^ (value >> size)
+        size += 1
+    return total & 1
+
+
+def early_first(me, i, devices):
+    if devices & (devices - 1) != 0:
+        return i
+    half = devices // 2
+    place = lax.rem(i, half)
+    late = i // half
+    return 2 * place + (bit_sum(place, devices) ^ bit_sum(me, devices) ^ late)
 
 
 def kernel(
@@ -230,9 +247,16 @@
     pl.semaphore_wait(barrier, devices - 1 + len(others) * devices)
     ahead = min(3, devices - 1)
 
+    def filter_start(i):
+        step = early_first(me, i, devices)
+
+        @pl.when(step > 0)
+        def _():
+            filter_copy(step).start()
+
     @pl.loop(0, ahead)
     def _(i):
-        filter_copy(1 + i).start()
+        filter_start(i)
 
     load_streams.wait()
 
@@ -246,9 +270,9 @@
     def _():
         halo_copy.start()
 
-    @pl.loop(ahead, devices - 1)
-    def _(i):
-        filter_copy(1 + i).start()
+    @pl.loop(ahead, devices)
+    def _(i):
+        filter_start(i)
 
     own_filter.start()
     for copy in loads:
@@ -286,13 +310,15 @@
         query[index] = found[0]
         skipped[index] = skip[:, at] * gated
 
-    @pl.loop(0, devices - 1)
-    def _(i):
-        step = 1 + i
+    @pl.loop(0, devices)
+    def _(i):
+        step = early_first(me, i, devices)
         features(partner(me, step, devices))
-        gated_copy(step).start()
-
-    features(me)
+
+        @pl.when(step > 0)
+        def _():
+            gated_copy(step).start()
+
     gated_in[me] = gated_out[me]
     cross_copy(0, query, query_in).start()
     cross_copy(1, skipped, skipped_in).start()
@@ -359,11 +385,10 @@
         for i in range(2):
             conv[:, group(g + i), :] = done[:, i * share : (i + 1) * share].reshape(devices, GROUP, share)
 
-    @pl.loop(1, devices)
+    @pl.loop(0, devices)
     def _(step):
-        conv_copy(step).start()
-
-    conv_copy(0).start()
+        conv_copy(devices - 1 - step).start()
+
 
     cross_copy(0, query, query_in).wait()
     cross_copy(1, skipped, skipped_in).wait()

time: 50.7 us -> 48.9 us (0.964)
  Pallas kernels: 47.9 us -> 46.4 us
    pallas_call x1, Pallas kernels: 47.9 us -> 46.4 us  [body_kernel(): call(streams, feat_taps[0], skip_gain, long_filter[0], jnp.asarray(short_...]
where the time goes in v2:
time: 48.9 us; the launch traced here: 48.3 us
  Pallas kernels  46.4 us (95%)
  local copies, waits for them, and re-layouts  1.88 us (4%)
    pallas_call x1, Pallas kernels, body_kernel(): call(streams, feat_taps[0], skip_gain, long_filter[0], jnp.asarray(short_...  46.4 us
    unnamed x1, local copies, waits for them, and re-layouts  1.88 us

profile of v2, /device:TPU:0, one launch (start us, length us, event | category | flops | bytes accessed | tf_op | source)
XLA Modules:
  0.0 48.3 jit_solution(14108647197377024023)
XLA Ops:
  0.0 46.4 %mixer.1 = bf16[128,2048]{1,0:T(8,128)(2,1)} custom-call(bf16[3,128,2048]{2,1,0:T(8,128)(2,1)} %bitcast.7, bf16[3,3,2048]{2,1,0:T(4,128)(2,1)} %bitcast.9, f32[1,2048]{1,0:T(1,128)} %skip_ref.1, bf16[128,2048]{1,0:T(8,128)(2,1)} %bitcast.8, bf16[2,512,256]{2,1,0:T(8,128)(2,1)} %constant.8.clone.short_ref, bf16[2,256,512]{2,1,0:T(8,128)(2,1)} %constant.9.clone.back_ref, ...), custom_call_target="tpu_custom_call" | custom-call | tf_op jit(solution)/shard_map/mixer/pallas_call | solution.py:478
  46.4 1.9 %copy.10 = bf16[1,128,2048]{2,1,0:T(8,128)(2,1)} copy(bf16[1,128,2048]{2,1,0:T(8,128)(2,1)} %bitcast.6) | data formatting | bytes 1048576
